TPU v7x, 128 devices: a whole 4x4x4 slice. The times are simulated.
128 devices in a mesh: row: 16 (over y_lo, x, core), col: 8 (over z, y_hi).
Axes of the slice: x: 4, y: 4 (y_hi: 2, y_lo: 2; y = y_hi * 2 + y_lo), z: 4, core: 2. Of those that a mesh axis runs over, the one named last changes fastest.
Arguments:
- velocity: float32 [2, 4096, 4096], P(None, 'row', 'col'), may hold values from -6 to 6
Outputs:
- restart: float32 [2, 8192, 8192], P(None, ('row', 'col'))
All inputs are finite; a program needn't handle non-finite values.
Results may differ from a plain program's by a relative error of at most 0.00007.
Values sent between devices are 32-bit elements; how exact they have to be, the bound alone decides.
A program may use at most 128 MiB of HBM per device.

v0:
```python
import functools

import jax
import jax.numpy as jnp
import ml_dtypes
import numpy as np
from jax import lax
from jax.experimental import pallas as pl
from jax.experimental.pallas import tpu as pltpu
from jax.sharding import PartitionSpec as P

OLD_N = 4096
RADIX = 16
BLOCK = 256
ROWS, COLS = 16, 8
MESH = pl.DeviceIdType.MESH
F32, BF16 = jnp.float32, jnp.bfloat16


def split_bf16(table):
    hi = table.astype(ml_dtypes.bfloat16)
    lo = (table - hi.astype(np.float64)).astype(ml_dtypes.bfloat16)
    return hi, lo


def phases(points, sign):
    angle = sign * 2.0 * np.pi * (np.arange(RADIX) - RADIX // 2)[:, None] * points[None, :] / OLD_N
    return np.stack([np.cos(angle), np.sin(angle)]).astype(np.float32)


def shift_kernel(points):
    s = points[None, :] - np.arange(BLOCK)[:, None]
    whole = s == np.round(s)
    safe = np.where(whole, 0.5, s)
    value = np.where(whole, (s == 0) * 1.0, np.sin(np.pi * safe) / (BLOCK * np.sin(np.pi * safe / BLOCK)))
    return value / RADIX


def dft4(parts, sign):
    (ar, ai), (br, bi), (cr, ci), (dr, di) = parts
    sr, si, er, ei = ar + cr, ai + ci, ar - cr, ai - ci
    tr, ti, fr, fi = br + dr, bi + di, br - dr, bi - di
    if sign < 0:
        fr, fi = -fr, -fi
    return [(sr + tr, si + ti), (er - fi, ei + fr), (sr - tr, si - ti), (er + fi, ei - fr)]


def dft16(parts, sign):
    half = [dft4([parts[4 * hi + lo] for hi in range(4)], sign) for lo in range(4)]
    out = [None] * 16
    for klo in range(4):
        column = []
        for lo in range(4):
            re, im = half[lo][klo]
            turn = lo * klo
            if turn == 4:
                re, im = (-im, re) if sign > 0 else (im, -re)
            elif turn:
                c = float(np.cos(2 * np.pi * turn / 16))
                s = float(sign * np.sin(2 * np.pi * turn / 16))
                if turn == 2:
                    re, im = (re - im) * c if sign > 0 else (re + im) * c, (im + re) * c if sign > 0 else (im - re) * c
                elif turn == 6:
                    re, im = (re * c - im * s, re * s + im * c)
                else:
                    re, im = (re * c - im * s, re * s + im * c)
            column.append((re, im))
        for khi, value in enumerate(dft4(column, sign)):
            out[klo + 4 * khi] = value
    return out


def drop_half_mode(re, im, alternate):
    tr = jnp.sum(re * alternate, axis=-1, keepdims=True) * (1.0 / BLOCK)
    ti = jnp.sum(im * alternate, axis=-1, keepdims=True) * (1.0 / BLOCK)
    return re - alternate * tr, im - alternate * ti


def turn_by(re, im, table, k, lanes):
    c, s = table[0, k : k + 1, lanes], table[1, k : k + 1, lanes]
    return re * c - im * s, re * s + im * c


def product(x, high, low):
    hi = x.astype(BF16)
    lo = (x - hi.astype(F32)).astype(BF16)
    dot = functools.partial(jnp.dot, preferred_element_type=F32)
    return dot(hi, high) + (dot(lo, high) + dot(hi, low))


def exchange_kernel(
    v_ref, pre_ref, post_ref, high_ref, low_ref, even_ref, odd_ref,
    turned, lines, spec, shifted, back, outbox, fixed, sums, all_sums, send_sem, recv_sem, token,
):
    r, c = lax.axis_index("row"), lax.axis_index("col")

    def row_peer(i):
        return lax.rem(r + i, ROWS)

    def col_peer(i):
        return lax.rem(c + i, COLS)

    barrier = pltpu.get_barrier_semaphore()

    @pl.loop(1, ROWS)
    def _(i):
        pl.semaphore_signal(barrier, inc=1, device_id={"row": row_peer(i), "col": c}, device_id_type=MESH)

    @pl.loop(1, COLS)
    def _(i):
        pl.semaphore_signal(barrier, inc=1, device_id={"row": r, "col": col_peer(i)}, device_id_type=MESH)

    @pl.loop(0, 8)
    def _(q):
        plane, tile = q // 4, q % 4
        lanes = pl.ds(pl.multiple_of(tile * 128, 128), 128)
        for half in range(2):
            block = v_ref[plane, half * 128 : half * 128 + 128, lanes].T
            turned[2 * q, :, half * 128 : half * 128 + 128] = block[:64]
            turned[2 * q + 1, :, half * 128 : half * 128 + 128] = block[64:]

    sign8 = 1.0 - 2.0 * (lax.broadcasted_iota(jnp.int32, (8, 512), 0) % 2).astype(F32)
    for plane in range(2):
        total = jnp.zeros((8, 512), F32)
        for g in range(32):
            total = total + v_ref[plane, 8 * g : 8 * g + 8, :]
        total = jnp.sum(total * sign8, axis=0, keepdims=True)
        for tile in range(4):
            sums[plane * 4 + tile : plane * 4 + tile + 1, :] = total[:, tile * 128 : tile * 128 + 128]

    lines[r] = turned[r]
    all_sums[r] = sums[...]

    pl.semaphore_wait(barrier, ROWS + COLS - 2)

    @pl.loop(1, COLS)
    def _(i):
        pl.semaphore_signal(token, inc=1, device_id={"row": r, "col": col_peer(i)}, device_id_type=MESH)

    @pl.loop(1, ROWS)
    def _(i):
        pltpu.make_async_remote_copy(
            sums, all_sums.at[r], send_sem.at[1], recv_sem.at[1],
            device_id={"row": row_peer(i), "col": c}, device_id_type=MESH,
        ).start()

    @pl.loop(1, ROWS)
    def _(i):
        pltpu.make_async_remote_copy(
            turned.at[row_peer(i)], lines.at[r], send_sem.at[0], recv_sem.at[0],
            device_id={"row": row_peer(i), "col": c}, device_id_type=MESH,
        ).start()

    others = all_sums.at[pl.ds(0, ROWS - 1)]
    pltpu.make_async_copy(others, others, recv_sem.at[1]).wait()
    nyquist = all_sums[0]
    for i in range(1, ROWS):
        nyquist = nyquist + all_sums[i]
    nyquist = nyquist * (1.0 / OLD_N)
    for plane in range(2):
        row = jnp.concatenate([nyquist[plane * 4 + tile : plane * 4 + tile + 1] for tile in range(4)], axis=1)
        correction = row * sign8
        for g in range(32):
            fixed[plane, 8 * g : 8 * g + 8, :] = v_ref[plane, 8 * g : 8 * g + 8, :] - correction

    def old_rows(peer):
        return fixed.at[:, pl.ds(pl.multiple_of(peer * 32, 32), 32), :]

    my_columns = even_ref.at[:, :, pl.ds(pl.multiple_of(c * 512, 512), 512)]

    @pl.loop(1, COLS)
    def _(i):
        pltpu.make_async_remote_copy(
            old_rows(col_peer(i)), my_columns, send_sem.at[2], recv_sem.at[2],
            device_id={"row": r, "col": col_peer(i)}, device_id_type=MESH,
        ).start()

    own_even = pltpu.make_async_copy(old_rows(c), my_columns, send_sem.at[4])
    own_even.start()

    others = lines.at[pl.ds(0, ROWS - 1)]
    pltpu.make_async_copy(others, others, recv_sem.at[0]).wait()

    alternate = 1.0 - 2.0 * (lax.broadcasted_iota(jnp.int32, (8, BLOCK), 1) % 2).astype(F32)

    @pl.loop(0, 4)
    def _(g):
        re_rows = pl.ds(pl.multiple_of(g * 8, 8), 8)
        im_rows = pl.ds(pl.multiple_of(g * 8 + 32, 8), 8)
        modes = dft16([(lines[b, re_rows, :], lines[b, im_rows, :]) for b in range(RADIX)], -1)
        modes[0] = drop_half_mode(*modes[0], alternate)
        for k in range(RADIX):
            re, im = turn_by(*modes[k], pre_ref, k, slice(None))
            spec[k, re_rows, :] = re
            spec[k, im_rows, :] = im

    @pl.loop(0, 4)
    def _(g):
        x = spec[pl.ds(g * 4, 4)].reshape(256, BLOCK)
        shifted[pl.ds(g * 4, 4)] = product(x, high_ref[...], low_ref[...]).reshape(4, 64, BLOCK)

    @pl.loop(0, 4)
    def _(g):
        re_rows = pl.ds(pl.multiple_of(g * 8, 8), 8)
        im_rows = pl.ds(pl.multiple_of(g * 8 + 32, 8), 8)
        for t in range(2):
            lanes = slice(t * 128, t * 128 + 128)
            modes = [
                turn_by(shifted[k, re_rows, lanes], shifted[k, im_rows, lanes], post_ref, k, lanes)
                for k in range(RADIX)
            ]
            points = dft16(modes, 1)
            for a in range(RADIX):
                back[a, t, re_rows, :] = points[a][0]
                back[a, t, im_rows, :] = points[a][1]

    pl.semaphore_wait(token, COLS - 1)

    @pl.loop(0, ROWS)
    def _(i):
        a = row_peer(i)
        outbox[a] = back[a].reshape(128, 128).T

        @pl.loop(0, COLS)
        def _(j):
            peer = col_peer(j)

            @pl.when(i + j > 0)
            def _():
                pltpu.make_async_remote_copy(
                    outbox.at[a, pl.ds(pl.multiple_of(peer * 16, 16), 16), :], odd_ref.at[r * COLS + c],
                    send_sem.at[3], recv_sem.at[3],
                    device_id={"row": a, "col": peer}, device_id_type=MESH,
                ).start()

    own_odd = pltpu.make_async_copy(
        outbox.at[r, pl.ds(pl.multiple_of(c * 16, 16), 16), :], odd_ref.at[r * COLS + c], send_sem.at[5]
    )
    own_odd.start()

    own_even.wait()
    own_odd.wait()
    sent = turned.at[pl.ds(0, ROWS - 1)]
    pltpu.make_async_copy(sent, sent, send_sem.at[0]).wait()
    sent = all_sums.at[pl.ds(0, ROWS - 1)]
    pltpu.make_async_copy(sent, sent, send_sem.at[1]).wait()
    sent = even_ref.at[:, :, pl.ds(0, 512 * (COLS - 1))]
    pltpu.make_async_copy(sent, sent, send_sem.at[2]).wait()
    pltpu.make_async_copy(sent, sent, recv_sem.at[2]).wait()
    sent = odd_ref.at[pl.ds(0, ROWS * COLS - 1)]
    pltpu.make_async_copy(sent, sent, send_sem.at[3]).wait()
    pltpu.make_async_copy(sent, sent, recv_sem.at[3]).wait()


def refine_kernel(even_ref, odd_ref, pre_ref, post_ref, high_ref, low_ref, out_ref, spec, shifted):
    g = pl.program_id(0)
    t = g // 2
    alternate = 1.0 - 2.0 * (lax.broadcasted_iota(jnp.int32, (8, BLOCK), 1) % 2).astype(F32)
    first = lax.broadcasted_iota(jnp.int32, (8, 128), 1) < 64

    def odd_block(plane, b):
        parts = []
        for h in range(2):
            zb = 4 * (b % 2) + 2 * h
            src = (plane * 8 + zb) * COLS + b // 2
            left = pltpu.roll(odd_ref[src], 64 * t, 1)
            right = pltpu.roll(odd_ref[src + COLS], 64 * (1 - t), 1)
            parts.append(jnp.where(first, left, right))
        return jnp.concatenate(parts, axis=1)

    for e in range(2):
        if e == 0:
            points = [tuple(even_ref[p, :, b * BLOCK : b * BLOCK + BLOCK] for p in range(2)) for b in range(RADIX)]
        else:
            points = [tuple(odd_block(p, b) for p in range(2)) for b in range(RADIX)]
        modes = dft16(points, -1)
        modes[0] = drop_half_mode(*modes[0], alternate)
        for k in range(RADIX):
            for p, value in enumerate(turn_by(*modes[k], pre_ref, k, slice(None))):
                for h in range(2):
                    rows = pl.ds(h * 512 + k * 32 + p * 16 + e, 8, stride=2)
                    spec[rows, :] = value[:, h * 128 : h * 128 + 128]
    for j in range(2):
        x = jnp.concatenate([spec[h * 512 + j * 256 : h * 512 + j * 256 + 256, :] for h in range(2)], axis=1)
        shifted[8 * j : 8 * j + 8] = product(x, high_ref[...], low_ref[...]).reshape(8, 32, 2 * BLOCK)
    for half in range(2):
        re_rows = slice(8 * half, 8 * half + 8)
        im_rows = slice(16 + 8 * half, 24 + 8 * half)

        @pl.loop(0, 4)
        def _(tile):
            lanes = pl.ds(pl.multiple_of(tile * 128, 128), 128)
            modes = [turn_by(shifted[k, re_rows, lanes], shifted[k, im_rows, lanes], post_ref, k, lanes) for k in range(RADIX)]
            values = dft16(modes, 1)
            for a in range(RADIX):
                where = pl.ds(pl.multiple_of(a * 2 * BLOCK + tile * 128, 128), 128)
                for p in range(2):
                    out_ref[p, re_rows, where] = values[a][p]


def on_device(velocity):
    old = np.arange(BLOCK, dtype=np.float64)
    lam = np.arange(BLOCK)
    order = 32 * ((lam % 128) // 16) + 16 * (lam // 128) + lam % 16
    both = np.arange(2 * BLOCK) / 2.0
    pre = phases(old, -1.0)
    post_y = phases(old[order] + 0.5, 1.0)
    post_z = phases(both, 1.0)
    high_y, low_y = split_bf16(shift_kernel(old[order] + 0.5))
    high_z, low_z = split_bf16(shift_kernel(both))
    vmem = pl.BlockSpec(memory_space=pltpu.VMEM)
    hbm = pl.BlockSpec(memory_space=pl.ANY)
    even, odd = pl.pallas_call(
        exchange_kernel,
        out_shape=(
            jax.ShapeDtypeStruct((2, 32, OLD_N), F32),
            jax.ShapeDtypeStruct((ROWS * COLS, 16, 128), F32),
        ),
        in_specs=[vmem] * 5,
        out_specs=(hbm, hbm),
        scratch_shapes=[
            pltpu.VMEM((ROWS, 64, BLOCK), F32),
            pltpu.VMEM((ROWS, 64, BLOCK), F32),
            pltpu.VMEM((RADIX, 64, BLOCK), F32),
            pltpu.VMEM((RADIX, 64, BLOCK), F32),
            pltpu.VMEM((RADIX, 2, 64, 128), F32),
            pltpu.VMEM((ROWS, 128, 128), F32),
            pltpu.VMEM((2, 256, 512), F32),
            pltpu.VMEM((8, 128), F32),
            pltpu.VMEM((ROWS, 8, 128), F32),
            pltpu.SemaphoreType.DMA((6,)),
            pltpu.SemaphoreType.DMA((4,)),
            pltpu.SemaphoreType.REGULAR,
        ],
        compiler_params=pltpu.CompilerParams(collective_id=0, has_side_effects=True, vmem_limit_bytes=48 << 20),
        name="exchange",
    )(velocity, jnp.asarray(pre), jnp.asarray(post_y), jnp.asarray(high_y), jnp.asarray(low_y))
    whole = lambda shape: pl.BlockSpec(shape, lambda g: (0,) * len(shape))
    return pl.pallas_call(
        refine_kernel,
        grid=(4,),
        out_shape=jax.ShapeDtypeStruct((2, 64, 2 * OLD_N), F32),
        in_specs=[
            pl.BlockSpec((2, 8, OLD_N), lambda g: (0, g, 0)),
            pl.BlockSpec((ROWS * COLS, 8, 128), lambda g: (0, g % 2, 0)),
            whole((2, RADIX, BLOCK)),
            whole((2, RADIX, 2 * BLOCK)),
            whole((BLOCK, 2 * BLOCK)),
            whole((BLOCK, 2 * BLOCK)),
        ],
        out_specs=pl.BlockSpec((2, 16, 2 * OLD_N), lambda g: (0, g, 0)),
        scratch_shapes=[
            pltpu.VMEM((1024, 128), F32),
            pltpu.VMEM((RADIX, 32, 2 * BLOCK), F32),
        ],
        compiler_params=pltpu.CompilerParams(vmem_limit_bytes=48 << 20),
        name="refine",
    )(even, odd, jnp.asarray(pre), jnp.asarray(post_z), jnp.asarray(high_z), jnp.asarray(low_z))


def solution(mesh):
    return jax.shard_map(
        on_device, mesh=mesh, in_specs=(P(None, "row", "col"),), out_specs=P(None, ("row", "col"), None), check_vma=False
    )
```

profile of v0, /device:TPU:1, one launch (start us, length us, event | category | flops | bytes accessed | tf_op | source)
XLA Modules:
  0.0 61.0 jit_solution(10480349037309124352)
XLA Ops:
  0.0 0.0 copy-start
  0.0 1.2 %copy-done = f32[2,256,512]{2,1,0:T(8,128)S(1)} copy-done((f32[2,256,512]{2,1,0:T(8,128)S(1)}, f32[2,256,512]{2,1,0:T(8,128)}, u32[]{:S(2)}) %copy-start) | copy-done | bytes 1048600
  1.2 0.0 copy-start.3
  1.2 0.8 %copy-done.3 = f32[2,16,256]{2,1,0:T(8,128)S(1)} copy-done((f32[2,16,256]{2,1,0:T(8,128)S(1)}, f32[2,16,256]{2,1,0:T(8,128)}, u32[]{:S(2)}) %copy-start.3) | copy-done | bytes 32792
  2.0 0.0 copy-start.4
  2.0 0.9 %copy-done.4 = bf16[256,256]{1,0:T(8,128)(2,1)S(1)} copy-done((bf16[256,256]{1,0:T(8,128)(2,1)S(1)}, bf16[256,256]{1,0:T(8,128)(2,1)}, u32[]{:S(2)}) %copy-start.4) | copy-done | bytes 131096
  2.9 0.0 copy-start.5
  2.9 0.9 %copy-done.5 = bf16[256,256]{1,0:T(8,128)(2,1)S(1)} copy-done((bf16[256,256]{1,0:T(8,128)(2,1)S(1)}, bf16[256,256]{1,0:T(8,128)(2,1)}, u32[]{:S(2)}) %copy-start.5) | copy-done | bytes 131096
  3.8 0.0 copy-start.7
  3.8 0.8 %copy-done.7 = f32[2,16,256]{2,1,0:T(8,128)S(1)} copy-done((f32[2,16,256]{2,1,0:T(8,128)S(1)}, f32[2,16,256]{2,1,0:T(8,128)}, u32[]{:S(2)}) %copy-start.7) | copy-done | bytes 32792
  4.6 46.2 %exchange.1 = (f32[2,32,4096]{2,1,0:T(8,128)S(1)}, f32[128,16,128]{2,1,0:T(8,128)S(1)}) custom-call(f32[2,256,512]{2,1,0:T(8,128)S(1)} %copy-done, f32[2,16,256]{2,1,0:T(8,128)S(1)} %copy-done.3, f32[2,16,256]{2,1,0:T(8,128)S(1)} %copy-done.7, bf16[256,256]{1,0:T(8,128)(2,1)S(1)} %copy-done.5, bf16[256,256]{1,0:T(8,128)(2,1)S(1)} %copy-done.4), custom_call_target="tpu_custom_call" | custom-call | tf_op jit(solution)/shard_map/exchange/pallas_call | solution.py:313
  50.8 0.0 copy-start.1
  50.8 0.9 %copy-done.1 = bf16[256,512]{1,0:T(8,128)(2,1)S(1)} copy-done((bf16[256,512]{1,0:T(8,128)(2,1)S(1)}, bf16[256,512]{1,0:T(8,128)(2,1)}, u32[]{:S(2)}) %copy-start.1) | copy-done | bytes 262168
  51.8 0.0 copy-start.2
  51.8 0.9 %copy-done.2 = bf16[256,512]{1,0:T(8,128)(2,1)S(1)} copy-done((bf16[256,512]{1,0:T(8,128)(2,1)S(1)}, bf16[256,512]{1,0:T(8,128)(2,1)}, u32[]{:S(2)}) %copy-start.2) | copy-done | bytes 262168
  52.7 0.0 copy-start.6
  52.7 0.8 %copy-done.6 = f32[2,16,512]{2,1,0:T(8,128)S(1)} copy-done((f32[2,16,512]{2,1,0:T(8,128)S(1)}, f32[2,16,512]{2,1,0:T(8,128)}, u32[]{:S(2)}) %copy-start.6) | copy-done | bytes 65560
  53.6 7.4 %refine.1 = f32[2,64,8192]{2,1,0:T(8,128)} custom-call(f32[2,32,4096]{2,1,0:T(8,128)S(1)} %get-tuple-element.7.even_ref, f32[128,16,128]{2,1,0:T(8,128)S(1)} %get-tuple-element.8.odd_ref, f32[2,16,256]{2,1,0:T(8,128)S(1)} %copy-done.3, f32[2,16,512]{2,1,0:T(8,128)S(1)} %copy-done.6, bf16[256,512]{1,0:T(8,128)(2,1)S(1)} %copy-done.2, ...), custom_call_target="tpu_custom_call" | custom-call | tf_op jit(solution)/shard_map/refine/pallas_call | solution.py:339
Async XLA Ops:
  0.0 1.2 %copy-start = (f32[2,256,512]{2,1,0:T(8,128)S(1)}, f32[2,256,512]{2,1,0:T(8,128)}, u32[]{:S(2)}) copy-start(f32[2,256,512]{2,1,0:T(8,128)} %v_ref.1) | copy-start | bytes 3145732
  1.2 0.8 %copy-start.3 = (f32[2,16,256]{2,1,0:T(8,128)S(1)}, f32[2,16,256]{2,1,0:T(8,128)}, u32[]{:S(2)}) copy-start(f32[2,16,256]{2,1,0:T(8,128)} %constant.14.clone.pre_ref) | copy-start | bytes 98308
  2.0 0.9 %copy-start.4 = (bf16[256,256]{1,0:T(8,128)(2,1)S(1)}, bf16[256,256]{1,0:T(8,128)(2,1)}, u32[]{:S(2)}) copy-start(bf16[256,256]{1,0:T(8,128)(2,1)} %constant.17.clone.low_ref) | copy-start | bytes 393220
  2.9 0.9 %copy-start.5 = (bf16[256,256]{1,0:T(8,128)(2,1)S(1)}, bf16[256,256]{1,0:T(8,128)(2,1)}, u32[]{:S(2)}) copy-start(bf16[256,256]{1,0:T(8,128)(2,1)} %constant.16.clone.high_ref) | copy-start | bytes 393220
  3.8 0.8 %copy-start.7 = (f32[2,16,256]{2,1,0:T(8,128)S(1)}, f32[2,16,256]{2,1,0:T(8,128)}, u32[]{:S(2)}) copy-start(f32[2,16,256]{2,1,0:T(8,128)} %constant.15.clone.post_ref) | copy-start | bytes 98308
  50.8 1.0 %copy-start.1 = (bf16[256,512]{1,0:T(8,128)(2,1)S(1)}, bf16[256,512]{1,0:T(8,128)(2,1)}, u32[]{:S(2)}) copy-start(bf16[256,512]{1,0:T(8,128)(2,1)} %constant.20.clone.low_ref) | copy-start | bytes 786436
  51.8 0.9 %copy-start.2 = (bf16[256,512]{1,0:T(8,128)(2,1)S(1)}, bf16[256,512]{1,0:T(8,128)(2,1)}, u32[]{:S(2)}) copy-start(bf16[256,512]{1,0:T(8,128)(2,1)} %constant.19.clone.high_ref) | copy-start | bytes 786436
  52.7 0.8 %copy-start.6 = (f32[2,16,512]{2,1,0:T(8,128)S(1)}, f32[2,16,512]{2,1,0:T(8,128)}, u32[]{:S(2)}) copy-start(f32[2,16,512]{2,1,0:T(8,128)} %constant.18.clone.post_ref) | copy-start | bytes 196612
where the time goes:
time: 62.1 us; the launch traced here: 61 us
  Pallas kernels  53.7 us (86%)
  local copies, waits for them, and re-layouts  7.28 us (12%)
    pallas_call x1, Pallas kernels, on_device(): pl.pallas_call(exchange_kernel, out_shape=(jax.ShapeDtypeStruct((2, 32, O...  46.2 us
    pallas_call x1, Pallas kernels, on_device(): pl.pallas_call(refine_kernel, grid=(4,), out_shape=jax.ShapeDtypeStruct((...  7.42 us
    unnamed x16, local copies, waits for them, and re-layouts  7.28 us

commit v1 on v0

v1 whole, which is shorter than its diff:
```python
import functools

import jax
import jax.numpy as jnp
import numpy as np
from jax import lax
from jax.experimental import pallas as pl
from jax.experimental.pallas import tpu as pltpu
from jax.sharding import PartitionSpec as P

OLD_N = 4096
RADIX = 16
BLOCK = 256
ROWS, COLS = 16, 8
MESH = pl.DeviceIdType.MESH
F32, BF16 = jnp.float32, jnp.bfloat16
PRE, POST_Y, POST_Z, TABLE_ROWS = 0, 64, 128, 256


def row_of(lam):
    return 32 * (lam % 128 // 16) + 16 * (lam // 128) + lam % 16


def fill_phases(table, base, tiles, halves, sign):
    for tile in range(tiles):
        k = lax.broadcasted_iota(jnp.int32, (RADIX, 128), 0) - RADIX // 2
        lane = lax.broadcasted_iota(jnp.int32, (RADIX, 128), 1) + tile * 128
        angle = (k * halves(lane)).astype(F32) * (sign * np.pi / OLD_N)
        table[base + tile * RADIX : base + tile * RADIX + RADIX, :] = jnp.cos(angle)
        table[base + (tiles + tile) * RADIX : base + (tiles + tile) * RADIX + RADIX, :] = jnp.sin(angle)


def fill_kernel(high, low, tiles, halves):
    for tile in range(tiles):

        @pl.loop(0, BLOCK // 32)
        def _(i):
            old = lax.broadcasted_iota(jnp.int32, (32, 128), 0) + i * 32
            twice = halves(lax.broadcasted_iota(jnp.int32, (32, 128), 1) + tile * 128) - 2 * old
            folded = jnp.where(twice > BLOCK, 2 * BLOCK - twice, jnp.where(twice < -BLOCK, -2 * BLOCK - twice, twice))
            odd = twice % 2 != 0
            sine = jnp.sin(jnp.where(odd, folded, 1).astype(F32) * (np.pi / (2 * BLOCK)))
            value = jnp.where((twice - 1) % 4 == 0, 1.0, -1.0) / (sine * (BLOCK * RADIX))
            value = jnp.where(odd, value, jnp.where(twice == 0, 1.0 / RADIX, 0.0))
            hi = value.astype(BF16)
            rows, lanes = pl.ds(pl.multiple_of(i * 32, 32), 32), slice(tile * 128, tile * 128 + 128)
            high[rows, lanes] = hi
            low[rows, lanes] = (value - hi.astype(F32)).astype(BF16)


def dft4(parts, sign):
    (ar, ai), (br, bi), (cr, ci), (dr, di) = parts
    sr, si, er, ei = ar + cr, ai + ci, ar - cr, ai - ci
    tr, ti, fr, fi = br + dr, bi + di, br - dr, bi - di
    if sign < 0:
        fr, fi = -fr, -fi
    return [(sr + tr, si + ti), (er - fi, ei + fr), (sr - tr, si - ti), (er + fi, ei - fr)]


def dft16(parts, sign):
    half = [dft4([parts[4 * hi + lo] for hi in range(4)], sign) for lo in range(4)]
    out = [None] * 16
    for klo in range(4):
        column = []
        for lo in range(4):
            re, im = half[lo][klo]
            turn = lo * klo
            if turn == 4:
                re, im = (-im, re) if sign > 0 else (im, -re)
            elif turn:
                c = float(np.cos(2 * np.pi * turn / 16))
                s = float(sign * np.sin(2 * np.pi * turn / 16))
                if turn == 2:
                    re, im = (re - im) * c if sign > 0 else (re + im) * c, (im + re) * c if sign > 0 else (im - re) * c
                elif turn == 6:
                    re, im = (re * c - im * s, re * s + im * c)
                else:
                    re, im = (re * c - im * s, re * s + im * c)
            column.append((re, im))
        for khi, value in enumerate(dft4(column, sign)):
            out[klo + 4 * khi] = value
    return out


def turn_by(re, im, table, base, tiles, tile, k):
    c = table[pl.ds(base + tile * RADIX + k, 1), :]
    s = table[pl.ds(base + (tiles + tile) * RADIX + k, 1), :]
    return re * c - im * s, re * s + im * c


def refine_rows(load, odd_row, table, high_ref, low_ref, spec, shifted, fine, finished=None):
    sign = 1.0 - 2.0 * (lax.broadcasted_iota(jnp.int32, (8, 128), 1) % 2).astype(F32)

    @pl.loop(0, 4)
    def _(g):
        first = []
        for h in range(2):
            modes = dft16([load(g, b, h) for b in range(RADIX)], -1)
            first.append(modes[0])
            for k in range(1, RADIX):
                for p, value in enumerate(turn_by(*modes[k], table, PRE, 2, h, k)):
                    spec[h, pl.ds(k * 64 + p * 32 + g * 8, 8), :] = value
        half = [
            sign * (jnp.sum((first[0][p] + first[1][p]) * sign, axis=-1, keepdims=True) * (1.0 / BLOCK)) for p in range(2)
        ]
        for h in range(2):
            for p, value in enumerate(turn_by(first[h][0] - half[0], first[h][1] - half[1], table, PRE, 2, h, 0)):
                spec[h, pl.ds(p * 32 + g * 8, 8), :] = value

    @pl.loop(0, 4)
    def _(j):
        rows = pl.ds(pl.multiple_of(j * 256, 256), 256)
        x = jnp.concatenate([spec[0, rows, :], spec[1, rows, :]], axis=1)
        shifted[rows, :] = product(x, high_ref[...], low_ref[...])

    @pl.loop(0, 4)
    def _(tile):
        lanes = pl.ds(pl.multiple_of(tile * 128, 128), 128)

        @pl.loop(0, 4)
        def _(g):
            modes = []
            for k in range(RADIX):
                re, im = (shifted[pl.ds(pl.multiple_of(k * 64 + p * 32 + g * 8, 8), 8), lanes] for p in range(2))
                modes.append(turn_by(re, im, table, POST_Z, 4, tile, k))
            values = dft16(modes, 1)
            for a in range(RADIX):
                for p in range(2):
                    fine[pl.ds(((p * RADIX + a) * 4 + tile) * 64 + g * 16 + odd_row, 8, stride=2), :] = values[a][p]

        if finished is not None:
            finished(tile)


def product(x, high, low):
    hi = x.astype(BF16)
    lo = (x - hi.astype(F32)).astype(BF16)
    dot = functools.partial(jnp.dot, preferred_element_type=F32)
    return dot(hi, high) + (dot(lo, high) + dot(hi, low))


def exchange_kernel(
    v_ref, fine, odd_ref, table, high_z, low_z, high_y, low_y, even_ref, spec_z, shifted_z,
    turned, lines, spec, shifted, back, outbox, fixed, sums, all_sums, send_sem, recv_sem, token,
):
    r, c = lax.axis_index("row"), lax.axis_index("col")

    def row_peer(i):
        return lax.rem(r + i, ROWS)

    def col_peer(i):
        return lax.rem(c + i, COLS)

    barrier = pltpu.get_barrier_semaphore()

    @pl.loop(1, ROWS)
    def _(i):
        pl.semaphore_signal(barrier, inc=1, device_id={"row": row_peer(i), "col": c}, device_id_type=MESH)

    @pl.loop(1, COLS)
    def _(i):
        pl.semaphore_signal(barrier, inc=1, device_id={"row": r, "col": col_peer(i)}, device_id_type=MESH)

    @pl.loop(0, 8)
    def _(q):
        plane, tile = q // 4, q % 4
        lanes = pl.ds(pl.multiple_of(tile * 128, 128), 128)
        for half in range(2):
            block = v_ref[plane, half * 128 : half * 128 + 128, lanes].T
            turned[2 * q, :, half * 128 : half * 128 + 128] = block[:64]
            turned[2 * q + 1, :, half * 128 : half * 128 + 128] = block[64:]

    sign8 = 1.0 - 2.0 * (lax.broadcasted_iota(jnp.int32, (8, 512), 0) % 2).astype(F32)
    for plane in range(2):
        total = jnp.zeros((8, 512), F32)
        for g in range(32):
            total = total + v_ref[plane, 8 * g : 8 * g + 8, :]
        total = jnp.sum(total * sign8, axis=0, keepdims=True)
        for tile in range(4):
            sums[plane * 4 + tile : plane * 4 + tile + 1, :] = total[:, tile * 128 : tile * 128 + 128]

    lines[r] = turned[r]
    all_sums[r] = sums[...]

    pl.semaphore_wait(barrier, ROWS + COLS - 2)

    @pl.loop(1, COLS)
    def _(i):
        pl.semaphore_signal(token, inc=1, device_id={"row": r, "col": col_peer(i)}, device_id_type=MESH)

    @pl.loop(1, ROWS)
    def _(i):
        pltpu.make_async_remote_copy(
            sums, all_sums.at[r], send_sem.at[1], recv_sem.at[1],
            device_id={"row": row_peer(i), "col": c}, device_id_type=MESH,
        ).start()

    @pl.loop(1, ROWS)
    def _(i):
        pltpu.make_async_remote_copy(
            turned.at[row_peer(i)], lines.at[r], send_sem.at[0], recv_sem.at[0],
            device_id={"row": row_peer(i), "col": c}, device_id_type=MESH,
        ).start()

    others = all_sums.at[pl.ds(0, ROWS - 1)]
    pltpu.make_async_copy(others, others, recv_sem.at[1]).wait()
    nyquist = all_sums[0]
    for i in range(1, ROWS):
        nyquist = nyquist + all_sums[i]
    nyquist = nyquist * (1.0 / OLD_N)
    for plane in range(2):
        row = jnp.concatenate([nyquist[plane * 4 + tile : plane * 4 + tile + 1] for tile in range(4)], axis=1)
        correction = row * sign8
        for g in range(32):
            fixed[plane, 8 * g : 8 * g + 8, :] = v_ref[plane, 8 * g : 8 * g + 8, :] - correction

    def old_rows(peer):
        return fixed.at[:, pl.ds(pl.multiple_of(peer * 32, 32), 32), :]

    my_columns = even_ref.at[:, :, pl.ds(pl.multiple_of(c * 512, 512), 512)]

    @pl.loop(1, COLS)
    def _(i):
        pltpu.make_async_remote_copy(
            old_rows(col_peer(i)), my_columns, send_sem.at[2], recv_sem.at[2],
            device_id={"row": r, "col": col_peer(i)}, device_id_type=MESH,
        ).start()

    own_even = pltpu.make_async_copy(old_rows(c), my_columns, send_sem.at[4])
    own_even.start()

    fill_phases(table, PRE, 2, lambda lane: 2 * lane, -1.0)
    fill_phases(table, POST_Y, 2, lambda lane: 2 * row_of(lane) + 1, 1.0)
    fill_phases(table, POST_Z, 4, lambda lane: lane, 1.0)
    fill_kernel(high_y, low_y, 2, lambda lane: 2 * row_of(lane) + 1)
    fill_kernel(high_z, low_z, 4, lambda lane: lane)

    others = lines.at[pl.ds(0, ROWS - 1)]
    pltpu.make_async_copy(others, others, recv_sem.at[0]).wait()

    sign = 1.0 - 2.0 * (lax.broadcasted_iota(jnp.int32, (8, 128), 1) % 2).astype(F32)

    @pl.loop(0, 4)
    def _(g):
        where = [pl.ds(pl.multiple_of(g * 8 + 32 * part, 8), 8) for part in range(2)]
        first = []
        for h in range(2):
            lanes = slice(h * 128, h * 128 + 128)
            modes = dft16([(lines[b, where[0], lanes], lines[b, where[1], lanes]) for b in range(RADIX)], -1)
            first.append(modes[0])
            for k in range(1, RADIX):
                for part, value in enumerate(turn_by(*modes[k], table, PRE, 2, h, k)):
                    spec[k, where[part], lanes] = value
        half = [
            sign * (jnp.sum((first[0][p] + first[1][p]) * sign, axis=-1, keepdims=True) * (1.0 / BLOCK)) for p in range(2)
        ]
        for h in range(2):
            lanes = slice(h * 128, h * 128 + 128)
            for part, value in enumerate(turn_by(first[h][0] - half[0], first[h][1] - half[1], table, PRE, 2, h, 0)):
                spec[0, where[part], lanes] = value

    @pl.loop(0, 4)
    def _(g):
        x = spec[pl.ds(g * 4, 4)].reshape(256, BLOCK)
        shifted[pl.ds(g * 4, 4)] = product(x, high_y[...], low_y[...]).reshape(4, 64, BLOCK)

    @pl.loop(0, 4)
    def _(g):
        where = [pl.ds(pl.multiple_of(g * 8 + 32 * part, 8), 8) for part in range(2)]
        for t in range(2):
            lanes = slice(t * 128, t * 128 + 128)
            modes = [
                turn_by(shifted[k, where[0], lanes], shifted[k, where[1], lanes], table, POST_Y, 2, t, k)
                for k in range(RADIX)
            ]
            points = dft16(modes, 1)
            for a in range(RADIX):
                for part in range(2):
                    back[a, t, where[part], :] = points[a][part]

    pl.semaphore_wait(token, COLS - 1)

    @pl.loop(0, ROWS)
    def _(i):
        a = row_peer(i)
        outbox[a] = back[a].reshape(128, 128).T

        @pl.loop(0, COLS)
        def _(j):
            peer = col_peer(j)

            @pl.when(i + j > 0)
            def _():
                pltpu.make_async_remote_copy(
                    outbox.at[a, pl.ds(pl.multiple_of(peer * 16, 16), 16), :], odd_ref.at[r * COLS + c],
                    send_sem.at[3], recv_sem.at[3],
                    device_id={"row": a, "col": peer}, device_id_type=MESH,
                ).start()

    own_odd = pltpu.make_async_copy(
        outbox.at[r, pl.ds(pl.multiple_of(c * 16, 16), 16), :], odd_ref.at[r * COLS + c], send_sem.at[5]
    )
    own_odd.start()

    own_even.wait()
    arrived = even_ref.at[:, :, pl.ds(0, 512 * (COLS - 1))]
    pltpu.make_async_copy(arrived, arrived, recv_sem.at[2]).wait()

    def load(g, b, h):
        rows = pl.ds(pl.multiple_of(g * 8, 8), 8)
        lanes = slice(b * BLOCK + h * 128, b * BLOCK + h * 128 + 128)
        return even_ref[0, rows, lanes], even_ref[1, rows, lanes]

    refine_rows(load, 0, table, high_z, low_z, spec_z, shifted_z, fine)

    own_odd.wait()
    sent = turned.at[pl.ds(0, ROWS - 1)]
    pltpu.make_async_copy(sent, sent, send_sem.at[0]).wait()
    sent = all_sums.at[pl.ds(0, ROWS - 1)]
    pltpu.make_async_copy(sent, sent, send_sem.at[1]).wait()
    sent = even_ref.at[:, :, pl.ds(0, 512 * (COLS - 1))]
    pltpu.make_async_copy(sent, sent, send_sem.at[2]).wait()
    sent = odd_ref.at[pl.ds(0, ROWS * COLS - 1)]
    pltpu.make_async_copy(sent, sent, send_sem.at[3]).wait()
    pltpu.make_async_copy(sent, sent, recv_sem.at[3]).wait()


def refine_kernel(fine_in, odd_ref, table, high_ref, low_ref, out_ref, fine, spec, shifted, sem):
    first = lax.broadcasted_iota(jnp.int32, (8, 128), 1) < 64

    def load(g, b, h):
        t, rows = g // 2, pl.ds(pl.multiple_of(8 * (g % 2), 8), 8)
        pair = []
        for plane in range(2):
            src = (plane * 8 + 4 * (b % 2) + 2 * h) * COLS + b // 2
            left = pltpu.roll(odd_ref[src, rows, :], 64 * t, 1)
            right = pltpu.roll(odd_ref[src + COLS, rows, :], 64 * (1 - t), 1)
            pair.append(jnp.where(first, left, right))
        return tuple(pair)

    def leave(tile):
        for p in range(2):

            @pl.loop(0, RADIX)
            def _(a):
                at = a * 4 + tile
                pltpu.make_async_copy(
                    fine.at[pl.ds(pl.multiple_of((p * 64 + at) * 64, 64), 64), :],
                    out_ref.at[p, :, pl.ds(pl.multiple_of(at * 128, 128), 128)],
                    sem,
                ).start()

    refine_rows(load, 1, table, high_ref, low_ref, spec, shifted, fine, leave)
    pltpu.make_async_copy(out_ref, out_ref, sem).wait()


def on_device(velocity):
    vmem = pl.BlockSpec(memory_space=pltpu.VMEM)
    hbm = pl.BlockSpec(memory_space=pltpu.HBM)
    fine, odd, phase, high, low = pl.pallas_call(
        exchange_kernel,
        out_shape=(
            jax.ShapeDtypeStruct((2 * 64 * 64, 128), F32),
            jax.ShapeDtypeStruct((ROWS * COLS, 16, 128), F32),
            jax.ShapeDtypeStruct((TABLE_ROWS, 128), F32),
            jax.ShapeDtypeStruct((BLOCK, 2 * BLOCK), BF16),
            jax.ShapeDtypeStruct((BLOCK, 2 * BLOCK), BF16),
        ),
        in_specs=[vmem],
        out_specs=(vmem,) * 5,
        scratch_shapes=[
            pltpu.VMEM((BLOCK, BLOCK), BF16),
            pltpu.VMEM((BLOCK, BLOCK), BF16),
            pltpu.VMEM((2, 32, OLD_N), F32),
            pltpu.VMEM((2, 1024, 128), F32),
            pltpu.VMEM((1024, 2 * BLOCK), F32),
            pltpu.VMEM((ROWS, 64, BLOCK), F32),
            pltpu.VMEM((ROWS, 64, BLOCK), F32),
            pltpu.VMEM((RADIX, 64, BLOCK), F32),
            pltpu.VMEM((RADIX, 64, BLOCK), F32),
            pltpu.VMEM((RADIX, 2, 64, 128), F32),
            pltpu.VMEM((ROWS, 128, 128), F32),
            pltpu.VMEM((2, 256, 512), F32),
            pltpu.VMEM((8, 128), F32),
            pltpu.VMEM((ROWS, 8, 128), F32),
            pltpu.SemaphoreType.DMA((8,)),
            pltpu.SemaphoreType.DMA((4,)),
            pltpu.SemaphoreType.REGULAR,
        ],
        compiler_params=pltpu.CompilerParams(collective_id=0, has_side_effects=True, vmem_limit_bytes=46 << 20),
        name="exchange",
    )(velocity)
    out, _ = pl.pallas_call(
        refine_kernel,
        out_shape=(
            jax.ShapeDtypeStruct((2, 64, 2 * OLD_N), F32),
            jax.ShapeDtypeStruct((2 * 64 * 64, 128), F32),
        ),
        in_specs=[vmem] * 5,
        out_specs=(hbm, vmem),
        scratch_shapes=[
            pltpu.VMEM((2, 1024, 128), F32),
            pltpu.VMEM((1024, 2 * BLOCK), F32),
            pltpu.SemaphoreType.DMA,
        ],
        input_output_aliases={0: 1},
        compiler_params=pltpu.CompilerParams(vmem_limit_bytes=40 << 20),
        name="refine",
    )(fine, odd, phase, high, low)
    return out


def solution(mesh):
    return jax.shard_map(
        on_device, mesh=mesh, in_specs=(P(None, "row", "col"),), out_specs=P(None, ("row", "col"), None), check_vma=False
    )
```

time: 62.1 us -> 54 us (0.87)
  local copies, waits for them, and re-layouts: 7.28 us -> 1.22 us
  Pallas kernels: 53.7 us -> 51.9 us
    unnamed x16 -> x2, local copies, waits for them, and re-layouts: 7.28 us -> 1.22 us
    pallas_call x2, Pallas kernels: 53.7 us -> 51.9 us  [the longest x1 46.3 us: on_device(): pl.pallas_call(exchange_kernel, out_shape=(jax.ShapeDtypeStruct((2 * 64 *...]
where the time goes in v1:
time: 54 us; the launch traced here: 53.2 us
  Pallas kernels  51.9 us (96%)
  local copies, waits for them, and re-layouts  1.22 us (2%)
    pallas_call x1, Pallas kernels, on_device(): pl.pallas_call(exchange_kernel, out_shape=(jax.ShapeDtypeStruct((2 * 64 *...  46.3 us
    pallas_call x1, Pallas kernels, on_device(): pl.pallas_call(refine_kernel, out_shape=(jax.ShapeDtypeStruct((2, 64, 2 *...  5.65 us
    unnamed x2, local copies, waits for them, and re-layouts  1.22 us

profile of v1, /device:TPU:1, one launch (start us, length us, event | category | flops | bytes accessed | tf_op | source)
XLA Modules:
  0.0 53.2 jit_solution(5484166917397230685)
XLA Ops:
  0.0 0.0 copy-start
  0.0 1.2 %copy-done = f32[2,256,512]{2,1,0:T(8,128)S(1)} copy-done((f32[2,256,512]{2,1,0:T(8,128)S(1)}, f32[2,256,512]{2,1,0:T(8,128)}, u32[]{:S(2)}) %copy-start) | copy-done | bytes 1048600
  1.2 46.3 %exchange.1 = (f32[8192,128]{1,0:T(8,128)S(1)}, f32[128,16,128]{2,1,0:T(8,128)S(1)}, f32[256,128]{1,0:T(8,128)S(1)}, bf16[256,512]{1,0:T(8,128)(2,1)S(1)}, bf16[256,512]{1,0:T(8,128)(2,1)S(1)}) custom-call(f32[2,256,512]{2,1,0:T(8,128)S(1)} %copy-done), custom_call_target="tpu_custom_call" | custom-call | tf_op jit(solution)/shard_map/exchange/pallas_call | solution.py:360
  47.5 5.7 %refine.1 = (f32[2,64,8192]{2,1,0:T(8,128)}, f32[8192,128]{1,0:T(8,128)S(1)}) custom-call(f32[8192,128]{1,0:T(8,128)S(1)} %get-tuple-element.11.fine_in, f32[128,16,128]{2,1,0:T(8,128)S(1)} %get-tuple-element.12.odd_ref, f32[256,128]{1,0:T(8,128)S(1)} %get-tuple-element.13.table, ...), custom_call_target="tpu_custom_call", output_to_operand_aliasing={{1}: (0, {})} | custom-call | tf_op jit(solution)/shard_map/refine/pallas_call | solution.py:393
Async XLA Ops:
  0.0 1.2 %copy-start = (f32[2,256,512]{2,1,0:T(8,128)S(1)}, f32[2,256,512]{2,1,0:T(8,128)}, u32[]{:S(2)}) copy-start(f32[2,256,512]{2,1,0:T(8,128)} %v_ref.1) | copy-start | bytes 3145732

commit v2 on v1

--- a/solution.py
+++ b/solution.py
@@ -30,7 +30,7 @@
         table[base + (tiles + tile) * RADIX : base + (tiles + tile) * RADIX + RADIX, :] = jnp.sin(angle)
 
 
-def fill_kernel(high, low, tiles, halves):
+def fill_kernel(stacked, tiles, halves):
     for tile in range(tiles):
 
         @pl.loop(0, BLOCK // 32)
@@ -43,9 +43,9 @@
             value = jnp.where((twice - 1) % 4 == 0, 1.0, -1.0) / (sine * (BLOCK * RADIX))
             value = jnp.where(odd, value, jnp.where(twice == 0, 1.0 / RADIX, 0.0))
             hi = value.astype(BF16)
-            rows, lanes = pl.ds(pl.multiple_of(i * 32, 32), 32), slice(tile * 128, tile * 128 + 128)
-            high[rows, lanes] = hi
-            low[rows, lanes] = (value - hi.astype(F32)).astype(BF16)
+            lanes = slice(tile * 128, tile * 128 + 128)
+            for part, half in enumerate((hi, hi, (value - hi.astype(F32)).astype(BF16))):
+                stacked[pl.ds(pl.multiple_of(part * BLOCK + i * 32, 32), 32), lanes] = half
 
 
 def dft4(parts, sign):
@@ -88,7 +88,7 @@
     return re * c - im * s, re * s + im * c
 
 
-def refine_rows(load, odd_row, table, high_ref, low_ref, spec, shifted, fine, finished=None):
+def refine_rows(load, odd_row, table, stacked, spec, shifted, fine):
     sign = 1.0 - 2.0 * (lax.broadcasted_iota(jnp.int32, (8, 128), 1) % 2).astype(F32)
 
     @pl.loop(0, 4)
@@ -111,7 +111,7 @@
     def _(j):
         rows = pl.ds(pl.multiple_of(j * 256, 256), 256)
         x = jnp.concatenate([spec[0, rows, :], spec[1, rows, :]], axis=1)
-        shifted[rows, :] = product(x, high_ref[...], low_ref[...])
+        shifted[rows, :] = product(x, stacked)
 
     @pl.loop(0, 4)
     def _(tile):
@@ -128,19 +128,15 @@
                 for p in range(2):
                     fine[pl.ds(((p * RADIX + a) * 4 + tile) * 64 + g * 16 + odd_row, 8, stride=2), :] = values[a][p]
 
-        if finished is not None:
-            finished(tile)
-
-
-def product(x, high, low):
+
+def product(x, stacked):
     hi = x.astype(BF16)
     lo = (x - hi.astype(F32)).astype(BF16)
-    dot = functools.partial(jnp.dot, preferred_element_type=F32)
-    return dot(hi, high) + (dot(lo, high) + dot(hi, low))
+    return jnp.dot(jnp.concatenate([hi, lo, hi], axis=1), stacked[...], preferred_element_type=F32)
 
 
 def exchange_kernel(
-    v_ref, fine, odd_ref, table, high_z, low_z, high_y, low_y, even_ref, spec_z, shifted_z,
+    v_ref, fine, odd_ref, table, kernel_z, kernel_y, even_ref, spec_z, shifted_z,
     turned, lines, spec, shifted, back, outbox, fixed, sums, all_sums, send_sem, recv_sem, token,
 ):
     r, c = lax.axis_index("row"), lax.axis_index("col")
@@ -232,8 +228,8 @@
     fill_phases(table, PRE, 2, lambda lane: 2 * lane, -1.0)
     fill_phases(table, POST_Y, 2, lambda lane: 2 * row_of(lane) + 1, 1.0)
     fill_phases(table, POST_Z, 4, lambda lane: lane, 1.0)
-    fill_kernel(high_y, low_y, 2, lambda lane: 2 * row_of(lane) + 1)
-    fill_kernel(high_z, low_z, 4, lambda lane: lane)
+    fill_kernel(kernel_y, 2, lambda lane: 2 * row_of(lane) + 1)
+    fill_kernel(kernel_z, 4, lambda lane: lane)
 
     others = lines.at[pl.ds(0, ROWS - 1)]
     pltpu.make_async_copy(others, others, recv_sem.at[0]).wait()
@@ -262,7 +258,7 @@
     @pl.loop(0, 4)
     def _(g):
         x = spec[pl.ds(g * 4, 4)].reshape(256, BLOCK)
-        shifted[pl.ds(g * 4, 4)] = product(x, high_y[...], low_y[...]).reshape(4, 64, BLOCK)
+        shifted[pl.ds(g * 4, 4)] = product(x, kernel_y).reshape(4, 64, BLOCK)
 
     @pl.loop(0, 4)
     def _(g):
@@ -311,7 +307,7 @@
         lanes = slice(b * BLOCK + h * 128, b * BLOCK + h * 128 + 128)
         return even_ref[0, rows, lanes], even_ref[1, rows, lanes]
 
-    refine_rows(load, 0, table, high_z, low_z, spec_z, shifted_z, fine)
+    refine_rows(load, 0, table, kernel_z, spec_z, shifted_z, fine)
 
     own_odd.wait()
     sent = turned.at[pl.ds(0, ROWS - 1)]
@@ -325,52 +321,83 @@
     pltpu.make_async_copy(sent, sent, recv_sem.at[3]).wait()
 
 
-def refine_kernel(fine_in, odd_ref, table, high_ref, low_ref, out_ref, fine, spec, shifted, sem):
+def refine_kernel(fine_in, odd_ref, table, stacked, out_ref, fine, spec, shifted, sem):
     first = lax.broadcasted_iota(jnp.int32, (8, 128), 1) < 64
+    sign = 1.0 - 2.0 * (lax.broadcasted_iota(jnp.int32, (8, 128), 1) % 2).astype(F32)
+    by_tile = fine.reshape(2, 64, 8, 8, 128)
 
     def load(g, b, h):
-        t, rows = g // 2, pl.ds(pl.multiple_of(8 * (g % 2), 8), 8)
+        t, rows = g // 2, slice(8 * (g % 2), 8 * (g % 2) + 8)
         pair = []
         for plane in range(2):
             src = (plane * 8 + 4 * (b % 2) + 2 * h) * COLS + b // 2
-            left = pltpu.roll(odd_ref[src, rows, :], 64 * t, 1)
-            right = pltpu.roll(odd_ref[src + COLS, rows, :], 64 * (1 - t), 1)
+            left, right = odd_ref[src, rows, :], odd_ref[src + COLS, rows, :]
+            if t:
+                left = pltpu.roll(left, 64, 1)
+            else:
+                right = pltpu.roll(right, 64, 1)
             pair.append(jnp.where(first, left, right))
         return tuple(pair)
 
-    def leave(tile):
+    def to_modes(g):
+        begin = []
+        for h in range(2):
+            modes = dft16([load(g, b, h) for b in range(RADIX)], -1)
+            begin.append(modes[0])
+            for k in range(1, RADIX):
+                for p, value in enumerate(turn_by(*modes[k], table, PRE, 2, h, k)):
+                    spec[g % 2, h, k * 16 + p * 8 : k * 16 + p * 8 + 8, :] = value
+        half = [
+            sign * (jnp.sum((begin[0][p] + begin[1][p]) * sign, axis=-1, keepdims=True) * (1.0 / BLOCK)) for p in range(2)
+        ]
+        for h in range(2):
+            for p, value in enumerate(turn_by(begin[h][0] - half[0], begin[h][1] - half[1], table, PRE, 2, h, 0)):
+                spec[g % 2, h, p * 8 : p * 8 + 8, :] = value
+
+    def shift(g):
+        x = jnp.concatenate([spec[g % 2, 0], spec[g % 2, 1]], axis=1)
+        shifted[g % 2] = product(x, stacked)
+
+    def to_points(g):
+        for tile in range(4):
+            lanes = slice(tile * 128, tile * 128 + 128)
+            modes = []
+            for k in range(RADIX):
+                re, im = (shifted[g % 2, k * 16 + p * 8 : k * 16 + p * 8 + 8, lanes] for p in range(2))
+                modes.append(turn_by(re, im, table, POST_Z, 4, tile, k))
+            values = dft16(modes, 1)
+            for a in range(RADIX):
+                for p in range(2):
+                    fine[pl.ds(((p * RADIX + a) * 4 + tile) * 64 + g * 16 + 1, 8, stride=2), :] = values[a][p]
         for p in range(2):
-
-            @pl.loop(0, RADIX)
-            def _(a):
-                at = a * 4 + tile
-                pltpu.make_async_copy(
-                    fine.at[pl.ds(pl.multiple_of((p * 64 + at) * 64, 64), 64), :],
-                    out_ref.at[p, :, pl.ds(pl.multiple_of(at * 128, 128), 128)],
-                    sem,
-                ).start()
-
-    refine_rows(load, 1, table, high_ref, low_ref, spec, shifted, fine, leave)
+            for tile in (2 * g, 2 * g + 1):
+                pltpu.make_async_copy(by_tile.at[p, :, tile], out_ref.at[p, tile], sem).start()
+
+    for step in range(6):
+        if step < 4:
+            to_modes(step)
+        if 1 <= step < 5:
+            shift(step - 1)
+        if step >= 2:
+            to_points(step - 2)
     pltpu.make_async_copy(out_ref, out_ref, sem).wait()
 
 
 def on_device(velocity):
     vmem = pl.BlockSpec(memory_space=pltpu.VMEM)
     hbm = pl.BlockSpec(memory_space=pltpu.HBM)
-    fine, odd, phase, high, low = pl.pallas_call(
+    fine, odd, phase, stacked = pl.pallas_call(
         exchange_kernel,
         out_shape=(
             jax.ShapeDtypeStruct((2 * 64 * 64, 128), F32),
             jax.ShapeDtypeStruct((ROWS * COLS, 16, 128), F32),
             jax.ShapeDtypeStruct((TABLE_ROWS, 128), F32),
-            jax.ShapeDtypeStruct((BLOCK, 2 * BLOCK), BF16),
-            jax.ShapeDtypeStruct((BLOCK, 2 * BLOCK), BF16),
+            jax.ShapeDtypeStruct((3 * BLOCK, 2 * BLOCK), BF16),
         ),
         in_specs=[vmem],
-        out_specs=(vmem,) * 5,
+        out_specs=(vmem,) * 4,
         scratch_shapes=[
-            pltpu.VMEM((BLOCK, BLOCK), BF16),
-            pltpu.VMEM((BLOCK, BLOCK), BF16),
+            pltpu.VMEM((3 * BLOCK, BLOCK), BF16),
             pltpu.VMEM((2, 32, OLD_N), F32),
             pltpu.VMEM((2, 1024, 128), F32),
             pltpu.VMEM((1024, 2 * BLOCK), F32),
@@ -393,21 +420,21 @@
     out, _ = pl.pallas_call(
         refine_kernel,
         out_shape=(
-            jax.ShapeDtypeStruct((2, 64, 2 * OLD_N), F32),
+            jax.ShapeDtypeStruct((2, 8, 64, 8, 128), F32),
             jax.ShapeDtypeStruct((2 * 64 * 64, 128), F32),
         ),
-        in_specs=[vmem] * 5,
+        in_specs=[vmem] * 4,
         out_specs=(hbm, vmem),
         scratch_shapes=[
-            pltpu.VMEM((2, 1024, 128), F32),
-            pltpu.VMEM((1024, 2 * BLOCK), F32),
+            pltpu.VMEM((2, 2, 256, 128), F32),
+            pltpu.VMEM((2, 256, 2 * BLOCK), F32),
             pltpu.SemaphoreType.DMA,
         ],
         input_output_aliases={0: 1},
         compiler_params=pltpu.CompilerParams(vmem_limit_bytes=40 << 20),
         name="refine",
-    )(fine, odd, phase, high, low)
-    return out
+    )(fine, odd, phase, stacked)
+    return out.transpose(0, 1, 3, 2, 4).reshape(2, 64, 2 * OLD_N)
 
 
 def solution(mesh):

time: 54 us -> 51.2 us (0.948)
  Pallas kernels: 51.9 us -> 49.1 us
    pallas_call x1, Pallas kernels: 5.65 us -> 2.88 us  [on_device(): pl.pallas_call(refine_kernel, out_shape=(jax.ShapeDtypeStruct((2, 8, 64,...]
where the time goes in v2:
time: 51.2 us; the launch traced here: 50.4 us
  Pallas kernels  49.1 us (96%)
  local copies, waits for them, and re-layouts  1.22 us (2%)
    pallas_call x1, Pallas kernels, on_device(): pl.pallas_call(exchange_kernel, out_shape=(jax.ShapeDtypeStruct((2 * 64 *...  46.3 us
    pallas_call x1, Pallas kernels, on_device(): pl.pallas_call(refine_kernel, out_shape=(jax.ShapeDtypeStruct((2, 8, 64,...  2.88 us
    unnamed x2, local copies, waits for them, and re-layouts  1.22 us

profile of v2, /device:TPU:1, one launch (start us, length us, event | category | flops | bytes accessed | tf_op | source)
XLA Modules:
  0.0 50.4 jit_solution(8673125376011761687)
XLA Ops:
  0.0 0.0 copy-start
  0.0 1.2 %copy-done = f32[2,256,512]{2,1,0:T(8,128)S(1)} copy-done((f32[2,256,512]{2,1,0:T(8,128)S(1)}, f32[2,256,512]{2,1,0:T(8,128)}, u32[]{:S(2)}) %copy-start) | copy-done | bytes 1048600
  1.2 46.3 %exchange.1 = (f32[8192,128]{1,0:T(8,128)S(1)}, f32[128,16,128]{2,1,0:T(8,128)S(1)}, f32[256,128]{1,0:T(8,128)S(1)}, bf16[768,512]{1,0:T(8,128)(2,1)S(1)}) custom-call(f32[2,256,512]{2,1,0:T(8,128)S(1)} %copy-done), custom_call_target="tpu_custom_call" | custom-call | tf_op jit(solution)/shard_map/exchange/pallas_call | solution.py:389
  47.5 2.9 %refine.1 = (f32[2,8,64,8,128]{4,3,2,1,0:T(8,128)}, f32[8192,128]{1,0:T(8,128)S(1)}) custom-call(f32[8192,128]{1,0:T(8,128)S(1)} %get-tuple-element.10.fine_in, f32[128,16,128]{2,1,0:T(8,128)S(1)} %get-tuple-element.11.odd_ref, f32[256,128]{1,0:T(8,128)S(1)} %get-tuple-element.12.table, ...), custom_call_target="tpu_custom_call", output_to_operand_aliasing={{1}: (0, {})} | custom-call | tf_op jit(solution)/shard_map/refine/pallas_call | solution.py:420
Async XLA Ops:
  0.0 1.2 %copy-start = (f32[2,256,512]{2,1,0:T(8,128)S(1)}, f32[2,256,512]{2,1,0:T(8,128)}, u32[]{:S(2)}) copy-start(f32[2,256,512]{2,1,0:T(8,128)} %v_ref.1) | copy-start | bytes 3145732

commit v3 on v2

--- a/solution.py
+++ b/solution.py
@@ -236,9 +236,8 @@
 
     sign = 1.0 - 2.0 * (lax.broadcasted_iota(jnp.int32, (8, 128), 1) % 2).astype(F32)
 
-    @pl.loop(0, 4)
-    def _(g):
-        where = [pl.ds(pl.multiple_of(g * 8 + 32 * part, 8), 8) for part in range(2)]
+    def to_modes(g):
+        where = [slice(g * 8 + 32 * part, g * 8 + 32 * part + 8) for part in range(2)]
         first = []
         for h in range(2):
             lanes = slice(h * 128, h * 128 + 128)
@@ -246,33 +245,36 @@
             first.append(modes[0])
             for k in range(1, RADIX):
                 for part, value in enumerate(turn_by(*modes[k], table, PRE, 2, h, k)):
-                    spec[k, where[part], lanes] = value
+                    spec[g % 2, h, k * 16 + part * 8 : k * 16 + part * 8 + 8, :] = value
         half = [
             sign * (jnp.sum((first[0][p] + first[1][p]) * sign, axis=-1, keepdims=True) * (1.0 / BLOCK)) for p in range(2)
         ]
         for h in range(2):
-            lanes = slice(h * 128, h * 128 + 128)
             for part, value in enumerate(turn_by(first[h][0] - half[0], first[h][1] - half[1], table, PRE, 2, h, 0)):
-                spec[0, where[part], lanes] = value
-
-    @pl.loop(0, 4)
-    def _(g):
-        x = spec[pl.ds(g * 4, 4)].reshape(256, BLOCK)
-        shifted[pl.ds(g * 4, 4)] = product(x, kernel_y).reshape(4, 64, BLOCK)
-
-    @pl.loop(0, 4)
-    def _(g):
-        where = [pl.ds(pl.multiple_of(g * 8 + 32 * part, 8), 8) for part in range(2)]
+                spec[g % 2, h, part * 8 : part * 8 + 8, :] = value
+
+    def shift(g):
+        shifted[g % 2] = product(jnp.concatenate([spec[g % 2, 0], spec[g % 2, 1]], axis=1), kernel_y)
+
+    def to_points(g):
         for t in range(2):
             lanes = slice(t * 128, t * 128 + 128)
-            modes = [
-                turn_by(shifted[k, where[0], lanes], shifted[k, where[1], lanes], table, POST_Y, 2, t, k)
-                for k in range(RADIX)
-            ]
+            modes = []
+            for k in range(RADIX):
+                re, im = (shifted[g % 2, k * 16 + part * 8 : k * 16 + part * 8 + 8, lanes] for part in range(2))
+                modes.append(turn_by(re, im, table, POST_Y, 2, t, k))
             points = dft16(modes, 1)
             for a in range(RADIX):
                 for part in range(2):
-                    back[a, t, where[part], :] = points[a][part]
+                    back[a, t, g * 8 + 32 * part : g * 8 + 32 * part + 8, :] = points[a][part]
+
+    for step in range(6):
+        if step < 4:
+            to_modes(step)
+        if 1 <= step < 5:
+            shift(step - 1)
+        if step >= 2:
+            to_points(step - 2)
 
     pl.semaphore_wait(token, COLS - 1)
 
@@ -324,7 +326,7 @@
 def refine_kernel(fine_in, odd_ref, table, stacked, out_ref, fine, spec, shifted, sem):
     first = lax.broadcasted_iota(jnp.int32, (8, 128), 1) < 64
     sign = 1.0 - 2.0 * (lax.broadcasted_iota(jnp.int32, (8, 128), 1) % 2).astype(F32)
-    by_tile = fine.reshape(2, 64, 8, 8, 128)
+    by_tile = fine.reshape(2, RADIX, 4, 8, 8, 128)
 
     def load(g, b, h):
         t, rows = g // 2, slice(8 * (g % 2), 8 * (g % 2) + 8)
@@ -369,9 +371,9 @@
             for a in range(RADIX):
                 for p in range(2):
                     fine[pl.ds(((p * RADIX + a) * 4 + tile) * 64 + g * 16 + 1, 8, stride=2), :] = values[a][p]
-        for p in range(2):
-            for tile in (2 * g, 2 * g + 1):
-                pltpu.make_async_copy(by_tile.at[p, :, tile], out_ref.at[p, tile], sem).start()
+            for p in range(2):
+                for eight in (2 * g, 2 * g + 1):
+                    pltpu.make_async_copy(by_tile.at[p, :, tile, eight], out_ref.at[p, eight, :, tile], sem).start()
 
     for step in range(6):
         if step < 4:
@@ -403,8 +405,8 @@
             pltpu.VMEM((1024, 2 * BLOCK), F32),
             pltpu.VMEM((ROWS, 64, BLOCK), F32),
             pltpu.VMEM((ROWS, 64, BLOCK), F32),
-            pltpu.VMEM((RADIX, 64, BLOCK), F32),
-            pltpu.VMEM((RADIX, 64, BLOCK), F32),
+            pltpu.VMEM((2, 2, 256, 128), F32),
+            pltpu.VMEM((2, 256, BLOCK), F32),
             pltpu.VMEM((RADIX, 2, 64, 128), F32),
             pltpu.VMEM((ROWS, 128, 128), F32),
             pltpu.VMEM((2, 256, 512), F32),
@@ -420,7 +422,7 @@
     out, _ = pl.pallas_call(
         refine_kernel,
         out_shape=(
-            jax.ShapeDtypeStruct((2, 8, 64, 8, 128), F32),
+            jax.ShapeDtypeStruct((2, 8, RADIX, 4, 8, 128), F32),
             jax.ShapeDtypeStruct((2 * 64 * 64, 128), F32),
         ),
         in_specs=[vmem] * 4,
@@ -434,7 +436,7 @@
         compiler_params=pltpu.CompilerParams(vmem_limit_bytes=40 << 20),
         name="refine",
     )(fine, odd, phase, stacked)
-    return out.transpose(0, 1, 3, 2, 4).reshape(2, 64, 2 * OLD_N)
+    return out.reshape(2, 8, 64, 8, 128).transpose(0, 1, 3, 2, 4).reshape(2, 64, 2 * OLD_N)
 
 
 def solution(mesh):

time: 51.2 us -> 50.8 us (level)
  no operation moved by 1% of the time
where the time goes in v3:
time: 50.8 us; the launch traced here: 50.3 us
  Pallas kernels  49 us (96%)
  local copies, waits for them, and re-layouts  1.22 us (2%)
    pallas_call x1, Pallas kernels, on_device(): pl.pallas_call(exchange_kernel, out_shape=(jax.ShapeDtypeStruct((2 * 64 *...  46.3 us
    pallas_call x1, Pallas kernels, on_device(): pl.pallas_call(refine_kernel, out_shape=(jax.ShapeDtypeStruct((2, 8, RADI...  2.77 us
    unnamed x2, local copies, waits for them, and re-layouts  1.22 us

profile of v3, /device:TPU:1, one launch (start us, length us, event | category | flops | bytes accessed | tf_op | source)
XLA Modules:
  0.0 50.3 jit_solution(5261766500372309140)
XLA Ops:
  0.0 0.0 copy-start
  0.0 1.2 %copy-done = f32[2,256,512]{2,1,0:T(8,128)S(1)} copy-done((f32[2,256,512]{2,1,0:T(8,128)S(1)}, f32[2,256,512]{2,1,0:T(8,128)}, u32[]{:S(2)}) %copy-start) | copy-done | bytes 1048600
  1.2 46.3 %exchange.1 = (f32[8192,128]{1,0:T(8,128)S(1)}, f32[128,16,128]{2,1,0:T(8,128)S(1)}, f32[256,128]{1,0:T(8,128)S(1)}, bf16[768,512]{1,0:T(8,128)(2,1)S(1)}) custom-call(f32[2,256,512]{2,1,0:T(8,128)S(1)} %copy-done), custom_call_target="tpu_custom_call" | custom-call | tf_op jit(solution)/shard_map/exchange/pallas_call | solution.py:391
  47.5 2.8 %refine.1 = (f32[2,8,16,4,8,128]{5,4,3,2,1,0:T(8,128)}, f32[8192,128]{1,0:T(8,128)S(1)}) custom-call(f32[8192,128]{1,0:T(8,128)S(1)} %get-tuple-element.10.fine_in, f32[128,16,128]{2,1,0:T(8,128)S(1)} %get-tuple-element.11.odd_ref, f32[256,128]{1,0:T(8,128)S(1)} %get-tuple-element.12.table, ...), custom_call_target="tpu_custom_call", output_to_operand_aliasing={{1}: (0, {})} | custom-call | tf_op jit(solution)/shard_map/refine/pallas_call | solution.py:422
Async XLA Ops:
  0.0 1.2 %copy-start = (f32[2,256,512]{2,1,0:T(8,128)S(1)}, f32[2,256,512]{2,1,0:T(8,128)}, u32[]{:S(2)}) copy-start(f32[2,256,512]{2,1,0:T(8,128)} %v_ref.1) | copy-start | bytes 3145732

commit v4 on v3

--- a/solution.py
+++ b/solution.py
@@ -180,10 +180,6 @@
 
     pl.semaphore_wait(barrier, ROWS + COLS - 2)
 
-    @pl.loop(1, COLS)
-    def _(i):
-        pl.semaphore_signal(token, inc=1, device_id={"row": r, "col": col_peer(i)}, device_id_type=MESH)
-
     @pl.loop(1, ROWS)
     def _(i):
         pltpu.make_async_remote_copy(
@@ -191,12 +187,18 @@
             device_id={"row": row_peer(i), "col": c}, device_id_type=MESH,
         ).start()
 
-    @pl.loop(1, ROWS)
-    def _(i):
+    @pl.loop(0, ROWS - 1)
+    def _(i):
+        half = lax.rem(r // 8 + 1 + lax.rem(i, 2), 2)
+        owner = half * 8 + lax.rem(r + (i + 1) // 2, 8)
         pltpu.make_async_remote_copy(
-            turned.at[row_peer(i)], lines.at[r], send_sem.at[0], recv_sem.at[0],
-            device_id={"row": row_peer(i), "col": c}, device_id_type=MESH,
+            turned.at[owner], lines.at[r], send_sem.at[0], recv_sem.at[0],
+            device_id={"row": owner, "col": c}, device_id_type=MESH,
         ).start()
+
+    @pl.loop(1, COLS)
+    def _(i):
+        pl.semaphore_signal(token, inc=1, device_id={"row": r, "col": col_peer(i)}, device_id_type=MESH)
 
     others = all_sums.at[pl.ds(0, ROWS - 1)]
     pltpu.make_async_copy(others, others, recv_sem.at[1]).wait()

time: 50.8 us -> 50.9 us (level)
  no operation moved by 1% of the time
where the time goes in v4:
time: 50.9 us; the launch traced here: 50.7 us
  Pallas kernels  49.5 us (97%)
  local copies, waits for them, and re-layouts  1.22 us (2%)
    pallas_call x1, Pallas kernels, on_device(): pl.pallas_call(exchange_kernel, out_shape=(jax.ShapeDtypeStruct((2 * 64 *...  46.7 us
    pallas_call x1, Pallas kernels, on_device(): pl.pallas_call(refine_kernel, out_shape=(jax.ShapeDtypeStruct((2, 8, RADI...  2.77 us
    unnamed x2, local copies, waits for them, and re-layouts  1.22 us

profile of v4, /device:TPU:1, one launch (start us, length us, event | category | flops | bytes accessed | tf_op | source)
XLA Modules:
  0.0 50.7 jit_solution(17039712045444742338)
XLA Ops:
  0.0 0.0 copy-start
  0.0 1.2 %copy-done = f32[2,256,512]{2,1,0:T(8,128)S(1)} copy-done((f32[2,256,512]{2,1,0:T(8,128)S(1)}, f32[2,256,512]{2,1,0:T(8,128)}, u32[]{:S(2)}) %copy-start) | copy-done | bytes 1048600
  1.2 46.7 %exchange.1 = (f32[8192,128]{1,0:T(8,128)S(1)}, f32[128,16,128]{2,1,0:T(8,128)S(1)}, f32[256,128]{1,0:T(8,128)S(1)}, bf16[768,512]{1,0:T(8,128)(2,1)S(1)}) custom-call(f32[2,256,512]{2,1,0:T(8,128)S(1)} %copy-done), custom_call_target="tpu_custom_call" | custom-call | tf_op jit(solution)/shard_map/exchange/pallas_call | solution.py:393
  48.0 2.8 %refine.1 = (f32[2,8,16,4,8,128]{5,4,3,2,1,0:T(8,128)}, f32[8192,128]{1,0:T(8,128)S(1)}) custom-call(f32[8192,128]{1,0:T(8,128)S(1)} %get-tuple-element.10.fine_in, f32[128,16,128]{2,1,0:T(8,128)S(1)} %get-tuple-element.11.odd_ref, f32[256,128]{1,0:T(8,128)S(1)} %get-tuple-element.12.table, ...), custom_call_target="tpu_custom_call", output_to_operand_aliasing={{1}: (0, {})} | custom-call | tf_op jit(solution)/shard_map/refine/pallas_call | solution.py:424
Async XLA Ops:
  0.0 1.2 %copy-start = (f32[2,256,512]{2,1,0:T(8,128)S(1)}, f32[2,256,512]{2,1,0:T(8,128)}, u32[]{:S(2)}) copy-start(f32[2,256,512]{2,1,0:T(8,128)} %v_ref.1) | copy-start | bytes 3145732
